TPU v7x, 256 devices: a whole 4x4x8 slice. The times are simulated.
256 devices in a mesh: row: 8 (over y, core), col: 32 (over z, x).
Axes of the slice: x: 4, y: 4, z: 8, core: 2. Of those that a mesh axis runs over, the one named last changes fastest.
Arguments:
- gradient: bfloat16 [9216, 36864], P(('row', 'col')), may hold values from -140 to 140
- weights: float32 [9216, 36864], P('row', 'col'), may hold values from -0.06 to 0.06
- row_old: float32 [9216], P(('row', 'col')), may hold values from 0.02 to 40, as said below
- col_old: float32 [36864], P('col'), may hold values from 0.02 to 40, as said below
Outputs:
- new_weights: float32 [9216, 36864], P('row', 'col')
- row_moment: float32 [9216], P(('row', 'col'))
- col_moment: float32 [36864], P('col')
Inputs may be any that keep to these rules, and one draw needn't show every extreme that they name: `row_old`: positive. `col_old`: positive.
All inputs are finite; a program needn't handle non-finite values.
Results may differ from a plain program's by a relative error of at most 0.0003.
Values may be sent and summed in bfloat16 or wider, within the bound.
A program may use at most 64 MiB of HBM per device.

v0:
```python
import jax
import jax.numpy as jnp
from jax import lax
from jax.sharding import PartitionSpec as P

D = 9216
FF = 36864


decay_rate = 0.8
tiny_value = 1e-30
clip_limit = 0.1
step_size = 0.25


def finish(values, row_vec, col_vec):
    update = values * lax.rsqrt(row_vec[:, None] * col_vec[None, :])
    square_sum = lax.psum(jnp.sum(update * update), ("row", "col"))
    factor = 1.0 / jnp.maximum(1.0, jnp.sqrt(square_sum / (D * FF)) / clip_limit)
    return (update, factor)


def local(gradient, weights, row_old, col_old):
    sub_rows = gradient.shape[0]
    col_index = lax.axis_index("col")
    blocked = lax.all_to_all(gradient, "col", split_axis=1, concat_axis=0, tiled=True)
    values = blocked.astype(jnp.float32)
    squares = values * values + tiny_value
    placed = lax.dynamic_update_slice(
        jnp.zeros((values.shape[0],), jnp.float32), decay_rate * row_old, (col_index * sub_rows,)
    )
    row_vec = lax.psum((1.0 - decay_rate) / FF * jnp.sum(squares, axis=1) + placed, "col")
    col_moment = decay_rate * col_old + (1.0 - decay_rate) / D * lax.psum(
        jnp.sum(squares, axis=0), "row"
    )
    row_moment = lax.dynamic_slice_in_dim(row_vec, col_index * sub_rows, sub_rows)
    update, factor = finish(values, row_vec, col_moment)
    new_weights = weights - step_size * factor * update
    return (new_weights, row_moment, col_moment)


def solution(mesh):
    in_specs = (P(("row", "col"), None), P("row", "col"), P(("row", "col")), P("col"))
    out_specs = (P("row", "col"), P(("row", "col")), P("col"))
    return jax.shard_map(local, mesh=mesh, in_specs=in_specs, out_specs=out_specs, check_vma=False)
```

profile of v0, /device:TPU:1, one launch (start us, length us, event | category | flops | bytes accessed | tf_op | source)
XLA Modules:
  0.0 267.6 jit_solution(5822567309338062912)
XLA Ops:
  0.6 2.2 copy.9
  2.9 0.2 slice
  3.1 2.5 copy.8
  5.5 0.0 copy-start.2
  5.6 0.0 copy-start.1
  5.6 12.0 %all-to-all-start = ((bf16[36,32,1152]{2,0,1:T(8,128)(2,1)}), bf16[36,32,1152]{2,0,1:T(8,128)(2,1)S(1)}, u32[]{:S(2)}, u32[]{:S(2)}) async-start(bf16[36,32,1152]{2,0,1:T(8,128)(2,1)} %copy.8), calls=%async_computation | async-start | bytes 5898240 | tf_op jit(solution)/shard_map/all_to_all | solution.py:26
  17.6 66.5 %all-to-all-done = bf16[36,32,1152]{2,0,1:T(8,128)(2,1)S(1)} async-done(((bf16[36,32,1152]{2,0,1:T(8,128)(2,1)}), bf16[36,32,1152]{2,0,1:T(8,128)(2,1)S(1)}, u32[]{:S(2)}, u32[]{:S(2)}) %all-to-all-start) | async-done | bytes 2654240 | tf_op jit(solution)/shard_map/all_to_all | solution.py:26
  84.1 1.6 fusion.1
  85.6 0.1 mul.79
  85.8 0.0 copy-done.2
  85.8 0.2 add_dynamic-update-slice_fusion
  86.0 59.3 %psum.21 = f32[1152]{0:T(1024)S(1)} all-reduce(f32[1152]{0:T(1024)S(1)} %add_dynamic-update-slice_fusion), channel_id=1, replica_groups=mesh['row'=8,'col'=32] {'col'}, use_global_device_ids=true, to_apply=%region_1.0 | all-reduce | flops 1152 | bytes 9216 | tf_op jit(solution)/shard_map/psum | solution.py:32
  145.2 28.1 %psum.22 = f32[1152]{0:T(1024)S(1)} all-reduce(f32[1152]{0:T(1024)S(1)} %get-tuple-element.4), channel_id=1, replica_groups=mesh['row'=8,'col'=32] {'row'}, use_global_device_ids=true, to_apply=%region_3.0 | all-reduce | flops 1152 | bytes 9216 | tf_op jit(solution)/shard_map/psum | solution.py:33
  173.4 0.1 mul.84
  173.5 0.0 copy-done.1
  173.5 0.0 copy-start
  173.5 3.1 %multiply_reduce_fusion = f32[]{:T(128)} fusion(bf16[36,32,1152]{2,0,1:T(8,128)(2,1)S(1)} %all-to-all-done, f32[1152]{0:T(1024)S(1)} %multiply_add_fusion.1, f32[32,36]{1,0:T(8,128)S(1)} %mul.84), kind=kLoop, calls=%fused_computation.1 | loop fusion | flops 6635519 | bytes 2663428 | tf_op jit(solution)/shard_map/reduce_sum | solution.py:18
  176.6 0.6 dynamic_slice.3
  177.2 72.6 %psum.23 = f32[]{:T(128)} all-reduce(f32[]{:T(128)} %multiply_reduce_fusion), channel_id=1, replica_groups=mesh['row'=8,'col'=32] {'row','col'}, use_global_device_ids=true, to_apply=%region_5.0 | all-reduce | flops 1 | bytes 8 | tf_op jit(solution)/shard_map/psum | solution.py:18
  250.6 2.9 %convert_bitcast_fusion = f32[32,36,1152]{2,1,0:T(8,128)} fusion(bf16[36,32,1152]{2,0,1:T(8,128)(2,1)S(1)} %all-to-all-done), kind=kLoop, calls=%fused_computation | loop fusion | flops 1327104 | bytes 7962624 | tf_op jit(solution)/shard_map/convert_element_type | solution.py:27
  253.5 6.7 %reshape.26 = f32[1152,1152]{1,0:T(8,128)} reshape(f32[32,36,1152]{2,1,0:T(8,128)} %convert_bitcast_fusion) | data formatting | bytes 10616832 | tf_op jit(solution)/shard_map/convert_element_type | solution.py:27
  260.2 0.0 copy-done
  260.2 7.4 %multiply_subtract_fusion = f32[1152,1152]{1,0:T(8,128)} fusion(f32[1152,1152]{1,0:T(8,128)} %param.5, f32[1152,1152]{1,0:T(8,128)} %reshape.26, f32[1152]{0:T(1024)S(1)} %multiply_add_fusion.1, f32[1152]{0:T(1024)S(1)} %psum.21, f32[]{:T(128)S(6)} %mul_shard_map.3), kind=kLoop, calls=%fused_computation.3 | loop fusion | flops 5308416 | bytes 15934468 | tf_op jit(solution)/shard_map/sub | solution.py:38
  (2 shorter events, 0.0 us)
Async XLA Ops:
  5.5 80.2 %copy-start.2 = (f32[36]{0:T(128)S(1)}, f32[36]{0:T(128)}, u32[]{:S(2)}) copy-start(f32[36]{0:T(128)} %param.6) | copy-start | bytes 436
  5.6 167.9 %copy-start.1 = (f32[1152]{0:T(1024)S(1)}, f32[1152]{0:T(1024)}, u32[]{:S(2)}) copy-start(f32[1152]{0:T(1024)} %param.7) | copy-start | bytes 13828
  5.6 78.5 %all-to-all-start = ((bf16[36,32,1152]{2,0,1:T(8,128)(2,1)}), bf16[36,32,1152]{2,0,1:T(8,128)(2,1)S(1)}, u32[]{:S(2)}, u32[]{:S(2)}) async-start(bf16[36,32,1152]{2,0,1:T(8,128)(2,1)} %copy.8), calls=%async_computation | async-start | bytes 5898240 | tf_op jit(solution)/shard_map/all_to_all | solution.py:26
  173.5 86.7 %copy-start = (f32[1152]{0:T(1024)}, f32[1152]{0:T(1024)S(1)}, u32[]{:S(2)}) copy-start(f32[1152]{0:T(1024)S(1)} %multiply_add_fusion.1) | copy-start | bytes 13828
where the time goes:
time: 268 us
  blocking collectives  160 us (60%)
  waiting for transfers between devices  66.5 us (25%)
  other arithmetic  15.2 us (6%)
  local copies, waits for them, and re-layouts  12.4 us (5%)
  starting transfers between devices  12 us (4%)
    psum x1, blocking collectives, finish(): square_sum = lax.psum(jnp.sum(update * update), ('row', 'col'))  72.6 us
    all_to_all x1, waiting for transfers between devices, local(): lax.all_to_all(gradient, 'col', split_axis=1, concat_axis=0, tiled=True)  66.5 us
    psum x1, blocking collectives, local(): lax.psum((1.0 - decay_rate) / FF * jnp.sum(squares, axis=1) + placed, 'col')  59.3 us
    psum x1, blocking collectives, local(): lax.psum(jnp.sum(squares, axis=0), 'row')  28.1 us
    all_to_all x1, starting transfers between devices, local(): lax.all_to_all(gradient, 'col', split_axis=1, concat_axis=0, tiled=True)  12 us
    sub x1, other arithmetic, local(): new_weights = weights - step_size * factor * update  7.4 us
    convert_element_type x1, local copies, waits for them, and re-layouts, local(): values = blocked.astype(jnp.float32)  6.68 us
  transfers between devices with their start and end apart: 1, of which 1 were waited for; matrix products, arithmetic and copies ran while one was open for 0% of the time, Pallas kernels for 0%

commit v1 on v0

v1 whole, which is shorter than its diff:
```python
import jax
import jax.numpy as jnp
from jax import lax
from jax.experimental import pallas as pl
from jax.experimental.pallas import tpu as pltpu
from jax.sharding import PartitionSpec as P

D = 9216
FF = 36864

decay_rate = 0.8
tiny_value = 1e-30
clip_limit = 0.1
step_size = 0.25

NZ, NX = 8, 4
NC = NZ * NX
NR = 8
SUB = D // NR // NC
MAIN = 32
REST = SUB - MAIN
W = FF // NC
CH = W // 128
PAIR = 2 * SUB
NP = NC // 2
F32 = jnp.float32
MESH = pl.DeviceIdType.MESH


def far_first(i):
    return 4 + (1 - 2 * (i % 2)) * ((i + 1) // 2)


def gather_kernel(
    g_hbm, row_old, col_old,
    u, scale, colm, rowm,
    gv, main, pack1, rest1, pack2, rest2, stage1, stage2, inv_out, inv_in, inv_col,
    sums, acc, total, totals,
    sem_g, main_s, main_r, inv_s, inv_r, r1_s, r1_r, r2_s, r2_r, sum_s, sum_r, tot_s, tot_r,
):
    row = lax.axis_index("row")
    me = lax.axis_index("col")
    z, x = me // NX, me % NX

    def peer(o):
        return lax.rem(z + o // NX, NZ) * NX + lax.rem(x + o % NX, NX)

    load = pltpu.make_async_copy(g_hbm, gv, sem_g)
    load.start()

    barrier = pltpu.get_barrier_semaphore()

    @pl.loop(1, NC)
    def _(o):
        pl.semaphore_signal(barrier, inc=1, device_id={"col": peer(o)}, device_id_type=MESH)

    @pl.loop(1, NR)
    def _(o):
        pl.semaphore_signal(barrier, inc=1, device_id={"row": lax.rem(row + o, NR)}, device_id_type=MESH)

    pl.semaphore_wait(barrier, NC - 1 + NR - 1)

    def block_cols(k):
        return pl.ds(pl.multiple_of(k * W, 128), W)

    def main_copy(k):
        return pltpu.make_async_remote_copy(
            src_ref=g_hbm.at[pl.ds(0, MAIN), block_cols(k)],
            dst_ref=main.at[me],
            send_sem=main_s.at[k],
            recv_sem=main_r.at[me],
            device_id={"col": k},
            device_id_type=MESH,
        )

    def main_wait(k):
        pltpu.make_async_copy(
            g_hbm.at[pl.ds(0, MAIN), pl.ds(0, W)], main.at[k], main_r.at[k]
        ).wait()

    def send_main(i):
        dz = far_first(i)

        @pl.loop(0, NX)
        def _(dx):
            k = lax.rem(z + dz, NZ) * NX + lax.rem(x + dx, NX)

            @pl.when(k != me)
            def _():
                main_copy(k).start()

    pltpu.make_async_copy(
        g_hbm.at[pl.ds(0, MAIN), block_cols(me)], main.at[me], main_r.at[me]
    ).start()

    @pl.loop(0, 3)
    def _(i):
        send_main(i)

    load.wait()

    def rest1_copy(zd):
        return pltpu.make_async_remote_copy(
            src_ref=pack1.at[zd],
            dst_ref=rest1.at[z],
            send_sem=r1_s.at[zd],
            recv_sem=r1_r.at[z],
            device_id={"col": zd * NX + x},
            device_id_type=MESH,
        )

    @pl.loop(0, NZ)
    def _(dz):
        zd = lax.rem(z + dz, NZ)
        for xd in range(NX):
            cols = pl.ds(pl.multiple_of((zd * NX + xd) * W, 128), W)
            stage1[xd * REST : (xd + 1) * REST, :] = gv[MAIN:SUB, cols].astype(F32)
        pack1[zd] = stage1[...].astype(jnp.bfloat16)

        @pl.when(dz != 0)
        def _():
            rest1_copy(zd).start()

        @pl.when(dz == 0)
        def _():
            rest1[zd] = stage1[...].astype(jnp.bfloat16)

    def add_up(k, carry):
        for c in range(CH):
            v = gv[:, pl.ds(pl.multiple_of(k * W + c * 128, 128), 128)].astype(F32)
            carry = carry + v * v
        return carry

    squares = lax.fori_loop(0, NC, add_up, jnp.zeros((SUB, 128), F32))
    sums_row = jnp.sum(squares, axis=1, keepdims=True)
    diagonal = lax.broadcasted_iota(jnp.int32, (SUB, 128), 0) == lax.broadcasted_iota(
        jnp.int32, (SUB, 128), 1
    )
    in_lanes = jnp.sum(
        jnp.where(diagonal, jnp.broadcast_to(sums_row, (SUB, 128)), 0.0), axis=0, keepdims=True
    )
    moment = decay_rate * row_old[...] + (1.0 - decay_rate) * (
        in_lanes[:, :SUB] * (1.0 / FF) + tiny_value
    )
    rowm[...] = moment
    inv_out[...] = jnp.zeros_like(inv_out)
    inv_out[:, :SUB] = lax.rsqrt(moment)
    inv_in[pl.ds(me, 1)] = inv_out[...].reshape(1, 1, 128)

    def inv_copy(k):
        return pltpu.make_async_remote_copy(
            src_ref=inv_out,
            dst_ref=inv_in.at[me],
            send_sem=inv_s.at[k],
            recv_sem=inv_r.at[me],
            device_id={"col": k},
            device_id_type=MESH,
        )

    @pl.loop(1, NC)
    def _(o):
        inv_copy(peer(o)).start()

    @pl.loop(3, NZ)
    def _(i):
        send_main(i)

    def rest2_copy(xd):
        return pltpu.make_async_remote_copy(
            src_ref=pack2.at[xd],
            dst_ref=rest2.at[x],
            send_sem=r2_s.at[xd],
            recv_sem=r2_r.at[x],
            device_id={"col": z * NX + xd},
            device_id_type=MESH,
        )

    @pl.loop(1, NZ)
    def _(o):
        zs = lax.rem(z + o, NZ)
        pltpu.make_async_copy(pack1.at[zs], rest1.at[zs], r1_r.at[zs]).wait()

    for xd in range(NX):
        for zs in range(NZ):
            stage2[xd, zs * REST : (zs + 1) * REST, :] = rest1[zs].astype(F32)[
                xd * REST : (xd + 1) * REST, :
            ]

    @pl.loop(0, NX)
    def _(xd):
        pack2[xd] = stage2[xd].astype(jnp.bfloat16)

        @pl.when(xd != x)
        def _():
            rest2_copy(xd).start()

        @pl.when(xd == x)
        def _():
            rest2[xd] = stage2[xd].astype(jnp.bfloat16)

    @pl.loop(0, NC)
    def _(k):
        @pl.when(k != me)
        def _():
            pltpu.make_async_copy(inv_out, inv_in.at[k], inv_r.at[k]).wait()

        line = inv_in[pl.ds(k, 1)].reshape(1, 128)
        column = jnp.sum(
            jnp.where(diagonal, jnp.broadcast_to(line, (SUB, 128)), 0.0), axis=1, keepdims=True
        )
        inv_col[k] = jnp.broadcast_to(column, (SUB, 128))

    acc[...] = jnp.zeros_like(acc)

    def take(zs):
        for h in range(NX // 2):
            for e in range(2):
                main_wait(zs * NX + 2 * h + e)
            for c in range(CH):
                lanes = slice(c * 128, (c + 1) * 128)
                squares = acc[0, :, lanes]
                scaled = acc[1, :, lanes]
                for e in range(2):
                    k = zs * NX + 2 * h + e
                    v = main[k, :, lanes].astype(F32)
                    w = v * inv_col[k, :MAIN, :]
                    u[zs * 2 + h, e * SUB : e * SUB + MAIN, lanes] = w
                    squares = squares + jnp.sum((v * v).reshape(MAIN // 8, 8, 128), axis=0)
                    scaled = scaled + jnp.sum((w * w).reshape(MAIN // 8, 8, 128), axis=0)
                acc[0, :, lanes] = squares
                acc[1, :, lanes] = scaled

    @pl.loop(0, NZ - 2)
    def _(i):
        take(lax.rem(z + NZ - far_first(i), NZ))

    @pl.loop(0, NX)
    def _(xs):
        @pl.when(xs != x)
        def _():
            pltpu.make_async_copy(pack2.at[xs], rest2.at[xs], r2_r.at[xs]).wait()

    for c in range(CH):
        lanes = slice(c * 128, (c + 1) * 128)
        squares = jnp.zeros((REST, 128), F32)
        scaled = jnp.zeros((REST, 128), F32)
        for xs in range(NX):
            rows = rest2[xs, :, lanes].astype(F32)
            for zs in range(NZ):
                v = rows[zs * REST : (zs + 1) * REST, :]
                w = v * inv_col[zs * NX + xs, MAIN:SUB, :]
                at = (xs % 2) * SUB + MAIN
                u[zs * 2 + xs // 2, at : at + REST, lanes] = w
                squares = squares + v * v
                scaled = scaled + w * w
        acc[0, :REST, lanes] = acc[0, :REST, lanes] + squares
        acc[1, :REST, lanes] = acc[1, :REST, lanes] + scaled

    @pl.loop(NZ - 2, NZ)
    def _(i):
        take(lax.rem(z + NZ - far_first(i), NZ))

    both = jnp.sum(acc[...], axis=1)
    mine = sums.at[row]
    mine[...] = both

    def sum_copy(r):
        return pltpu.make_async_remote_copy(
            src_ref=sums.at[row],
            dst_ref=sums.at[row],
            send_sem=sum_s.at[r],
            recv_sem=sum_r.at[row],
            device_id={"row": r},
            device_id_type=MESH,
        )

    @pl.loop(1, NR)
    def _(o):
        sum_copy(lax.rem(row + o, NR)).start()

    @pl.loop(1, NR)
    def _(o):
        r = lax.rem(row + o, NR)
        pltpu.make_async_copy(sums.at[r], sums.at[r], sum_r.at[r]).wait()

    added = jnp.sum(sums[...], axis=0)
    moments = decay_rate * col_old[...] + (1.0 - decay_rate) * (
        added[0:1, :] * (1.0 / D) + tiny_value
    )
    colm[...] = moments
    inverse = lax.rsqrt(moments)
    part = added[1:2, :] * (inverse * inverse)
    line = part[:, 0:128]
    for c in range(1, CH):
        line = line + part[:, c * 128 : (c + 1) * 128]
    total[...] = line
    totals[pl.ds(me, 1)] = line.reshape(1, 1, 128)

    def total_copy(k):
        return pltpu.make_async_remote_copy(
            src_ref=total,
            dst_ref=totals.at[me],
            send_sem=tot_s.at[k],
            recv_sem=tot_r.at[me],
            device_id={"col": k},
            device_id_type=MESH,
        )

    @pl.loop(1, NC)
    def _(o):
        total_copy(peer(o)).start()

    @pl.loop(1, NC)
    def _(o):
        k = peer(o)
        pltpu.make_async_copy(total, totals.at[k], tot_r.at[k]).wait()

    square_sum = jnp.sum(jnp.sum(totals[...], axis=0), axis=1, keepdims=True)
    factor = 1.0 / jnp.maximum(1.0, jnp.sqrt(square_sum / (D * FF)) / clip_limit)
    scale[...] = (step_size * factor) * inverse

    @pl.loop(1, NC)
    def _(o):
        k = peer(o)
        main_copy(k).wait_send()
        inv_copy(k).wait_send()
        total_copy(k).wait_send()

    @pl.loop(1, NR)
    def _(o):
        sum_copy(lax.rem(row + o, NR)).wait_send()

    @pl.loop(1, NZ)
    def _(o):
        rest1_copy(lax.rem(z + o, NZ)).wait_send()

    @pl.loop(1, NX)
    def _(o):
        rest2_copy(lax.rem(x + o, NX)).wait_send()


def apply_kernel(u, weights, scale, colm_in, rowm_in, out_hbm, colm, rowm, done, sem):
    colm[...] = colm_in[...]
    rowm[...] = rowm_in[...]

    @pl.loop(0, NP)
    def _(p):
        for c in range(CH):
            lanes = slice(c * 128, (c + 1) * 128)
            done[p, :, lanes] = weights[p, :, lanes] - scale[:, lanes] * u[p, :, lanes]
        pltpu.make_async_copy(done.at[p], out_hbm.at[p], sem.at[p]).start()

    @pl.loop(0, NP)
    def _(p):
        pltpu.make_async_copy(done.at[p], out_hbm.at[p], sem.at[p]).wait()


def local(gradient, weights, row_old, col_old):
    vmem = pl.BlockSpec(memory_space=pltpu.VMEM)
    bf16 = jnp.bfloat16
    dma = pltpu.SemaphoreType.DMA
    u, scale, colm, rowm = pl.pallas_call(
        gather_kernel,
        out_shape=(
            pltpu.VMEM((NP, PAIR, W), F32),
            pltpu.VMEM((1, W), F32),
            pltpu.VMEM((1, W), F32),
            pltpu.VMEM((1, SUB), F32),
        ),
        in_specs=[pl.BlockSpec(memory_space=pltpu.HBM), vmem, vmem],
        out_specs=(vmem, vmem, vmem, vmem),
        scratch_shapes=[
            pltpu.VMEM((SUB, FF), bf16),
            pltpu.VMEM((NC, MAIN, W), bf16),
            pltpu.VMEM((NZ, NX * REST, W), bf16),
            pltpu.VMEM((NZ, NX * REST, W), bf16),
            pltpu.VMEM((NX, NZ * REST, W), bf16),
            pltpu.VMEM((NX, NZ * REST, W), bf16),
            pltpu.VMEM((NX * REST, W), F32),
            pltpu.VMEM((NX, NZ * REST, W), F32),
            pltpu.VMEM((1, 128), F32),
            pltpu.VMEM((NC, 1, 128), F32),
            pltpu.VMEM((NC, SUB, 128), F32),
            pltpu.VMEM((NR, 2, W), F32),
            pltpu.VMEM((2, 8, W), F32),
            pltpu.VMEM((1, 128), F32),
            pltpu.VMEM((NC, 1, 128), F32),
            dma, dma((NC,)), dma((NC,)), dma((NC,)), dma((NC,)),
            dma((NZ,)), dma((NZ,)), dma((NX,)), dma((NX,)),
            dma((NR,)), dma((NR,)), dma((NC,)), dma((NC,)),
        ],
        compiler_params=pltpu.CompilerParams(
            collective_id=0, has_side_effects=True, vmem_limit_bytes=24 * 2**20
        ),
        cost_estimate=pl.CostEstimate(
            flops=8 * SUB * FF, bytes_accessed=4 * SUB * FF, transcendentals=0
        ),
        name="gather_kernel",
    )(gradient, row_old.reshape(1, SUB), col_old.reshape(1, W))
    weights = pltpu.with_memory_space_constraint(weights.reshape(NP, PAIR, W), pltpu.VMEM)
    new_weights, colm, rowm = pl.pallas_call(
        apply_kernel,
        out_shape=(
            jax.ShapeDtypeStruct((NP, PAIR, W), F32),
            jax.ShapeDtypeStruct((1, W), F32),
            jax.ShapeDtypeStruct((1, SUB), F32),
        ),
        in_specs=[vmem] * 5,
        out_specs=(pl.BlockSpec(memory_space=pltpu.HBM), vmem, vmem),
        scratch_shapes=[pltpu.VMEM((NP, PAIR, W), F32), dma((NP,))],
        compiler_params=pltpu.CompilerParams(vmem_limit_bytes=16 * 2**20),
        cost_estimate=pl.CostEstimate(
            flops=2 * SUB * FF, bytes_accessed=4 * SUB * FF, transcendentals=0
        ),
        name="apply_kernel",
    )(u, weights, scale, colm, rowm)
    return (new_weights.reshape(SUB * NC, W), rowm.reshape(SUB), colm.reshape(W))


def solution(mesh):
    in_specs = (P(("row", "col"), None), P("row", "col"), P(("row", "col")), P("col"))
    out_specs = (P("row", "col"), P(("row", "col")), P("col"))
    return jax.shard_map(local, mesh=mesh, in_specs=in_specs, out_specs=out_specs, check_vma=False)
```

time: 268 us -> 97.3 us (0.36)
  blocking collectives: 160 us -> 0 us
  Pallas kernels: 0 us -> 90.1 us
  waiting for transfers between devices: 66.5 us -> 0 us
  other arithmetic: 15.2 us -> 0.62 us
  starting transfers between devices: 12 us -> 0 us
  local copies, waits for them, and re-layouts: 12.4 us -> 5.69 us
    psum x3 -> x0, blocking collectives: 160 us -> none  [the longest x1 72.6 us: finish(): square_sum = lax.psum(jnp.sum(update * update), ('row', 'col'))]
    pallas_call x0 -> x2, Pallas kernels: none -> 90.1 us  [the longest x1 87.1 us: local(): pl.pallas_call(gather_kernel, out_shape=(pltpu.VMEM((NP, PAIR, W), F32),...]
    all_to_all x1 -> x0, waiting for transfers between devices: 66.5 us -> none  [local(): lax.all_to_all(gradient, 'col', split_axis=1, concat_axis=0, tiled=True)]
    all_to_all x1 -> x0, starting transfers between devices: 12 us -> none  [local(): lax.all_to_all(gradient, 'col', split_axis=1, concat_axis=0, tiled=True)]
    sub x1 -> x0, other arithmetic: 7.4 us -> none  [local(): new_weights = weights - step_size * factor * update]
    convert_element_type x1 -> x0, local copies, waits for them, and re-layouts: 6.68 us -> none  [local(): values = blocked.astype(jnp.float32)]
    reduce_sum x2 -> x0, other arithmetic: 4.71 us -> none  [the longest x1 3.14 us: finish(): square_sum = lax.psum(jnp.sum(update * update), ('row', 'col'))]
    convert_element_type x1 -> x0, other arithmetic: 2.9 us -> none  [local(): values = blocked.astype(jnp.float32)]
  transfers between devices with their start and end apart: 1 -> 0, of which waited for: 1 -> 0; matrix products, arithmetic and copies ran while one was open for 0% -> 0% of each run, Pallas kernels for 0% -> 0%
where the time goes in v1:
time: 97.3 us; the launch traced here: 97.1 us
  Pallas kernels  90.1 us (93%)
  local copies, waits for them, and re-layouts  5.69 us (6%)
    pallas_call x1, Pallas kernels, local(): pl.pallas_call(gather_kernel, out_shape=(pltpu.VMEM((NP, PAIR, W), F32),...  87.1 us
    unnamed x6, local copies, waits for them, and re-layouts  4.99 us
    pallas_call x1, Pallas kernels, local(): pl.pallas_call(apply_kernel, out_shape=(jax.ShapeDtypeStruct((NP, PAIR, W...  3.04 us

profile of v1, /device:TPU:1, one launch (start us, length us, event | category | flops | bytes accessed | tf_op | source)
XLA Modules:
  0.0 97.1 jit_solution(4681099641505951859)
XLA Ops:
  0.6 0.7 reshape.25.col_old
  1.3 0.0 copy-start.1
  1.3 1.8 %copy-done.1 = bf16[36,36864]{1,0:T(8,128)(2,1)S(1)} copy-done((bf16[36,36864]{1,0:T(8,128)(2,1)S(1)}, bf16[36,36864]{1,0:T(8,128)(2,1)}, u32[]{:S(2)}) %copy-start.1) | copy-done | bytes 2654232
  3.2 0.0 copy-start.2
  3.2 0.7 copy-done.2
  3.8 87.1 %gather_kernel.1 = (f32[16,72,1152]{2,1,0:T(8,128)S(1)}, f32[1,1152]{1,0:T(1,128)S(1)}, f32[1,1152]{1,0:T(1,128)S(1)}, f32[1,36]{1,0:T(1,128)S(1)}) custom-call(bf16[36,36864]{1,0:T(8,128)(2,1)S(1)} %copy-done.1, f32[1,36]{1,0:T(1,128)S(1)} %bitcast.5, f32[1,1152]{1,0:T(1,128)S(1)} %reshape.25.col_old), custom_call_target="tpu_custom_call" | custom-call | flops 10616832 | bytes 5308416 | tf_op jit(solution)/shard_map/gather_kernel/pallas_call | solution.py:362
  90.9 0.0 copy-start
  90.9 2.5 %copy-done = f32[1152,1152]{1,0:T(8,128)S(1)} copy-done((f32[1152,1152]{1,0:T(8,128)S(1)}, f32[1152,1152]{1,0:T(8,128)}, u32[]{:S(2)}) %copy-start) | copy-done | bytes 5308440
  93.4 3.0 %apply_kernel.1 = (f32[16,72,1152]{2,1,0:T(8,128)}, f32[1,1152]{1,0:T(1,128)S(1)}, f32[1,36]{1,0:T(1,128)}) custom-call(f32[16,72,1152]{2,1,0:T(8,128)S(1)} %get-tuple-element.10.u, f32[16,72,1152]{2,1,0:T(8,128)S(1)} %bitcast.4, f32[1,1152]{1,0:T(1,128)S(1)} %get-tuple-element.11.scale, f32[1,1152]{1,0:T(1,128)S(1)} %get-tuple-element.12.colm_in, ...), custom_call_target="tpu_custom_call" | custom-call | flops 2654208 | bytes 5308416 | tf_op jit(solution)/shard_map/apply_kernel/pallas_call | solution.py:401
  96.4 0.6 reduce
Async XLA Ops:
  1.3 1.8 %copy-start.1 = (bf16[36,36864]{1,0:T(8,128)(2,1)S(1)}, bf16[36,36864]{1,0:T(8,128)(2,1)}, u32[]{:S(2)}) copy-start(bf16[36,36864]{1,0:T(8,128)(2,1)} %g_hbm.1) | copy-start | bytes 7962628
  3.2 0.7 copy-start.2
  90.9 2.5 %copy-start = (f32[1152,1152]{1,0:T(8,128)S(1)}, f32[1152,1152]{1,0:T(8,128)}, u32[]{:S(2)}) copy-start(f32[1152,1152]{1,0:T(8,128)} %param.5) | copy-start | bytes 15925252

commit v2 on v0

v2 whole, which is shorter than its diff:
```python
import jax
import jax.numpy as jnp
from jax import lax
from jax.experimental import pallas as pl
from jax.experimental.pallas import tpu as pltpu
from jax.sharding import PartitionSpec as P

D = 9216
FF = 36864

decay_rate = 0.8
tiny_value = 1e-30
clip_limit = 0.1
step_size = 0.25

NZ, NX = 8, 4
NC = NZ * NX
NR = 8
NL = NR * NX
SUB = D // NR // NC
MAIN = 32
REST = SUB - MAIN
W = FF // NC
CH = W // 128
PAIR = 2 * SUB
NP = NC // 2
STRIDE = 13
BATCHES = (6, 5, 5, 5, 5, 5)
F32 = jnp.float32
BF16 = jnp.bfloat16
MESH = pl.DeviceIdType.MESH


def lane_slices():
    return [(c, slice(c * 128, (c + 1) * 128)) for c in range(CH)]


def gather_kernel(
    g_hbm, w_hbm, row_hbm, col_hbm,
    done, colm, rowm,
    weights, row_old, col_old, gv, main, pack1, rest1, pack2, rest2, stage1, stage2,
    inv_out, inv_in, inv_col, part, parts, zsums, moments, inverse, lines, zlines,
    sem_g, sem_w, sem_old, main_s, main_r, inv_s, inv_r, r1_s, r1_r, r2_s, r2_r, small_s, small_r,
):
    row = lax.axis_index("row")
    me = lax.axis_index("col")
    z, x = me // NX, me % NX
    here = row * NX + x

    def peer(o):
        return lax.rem(z + o // NX, NZ) * NX + lax.rem(x + o % NX, NX)

    def source(o):
        return lax.rem(z + NZ - o // NX, NZ) * NX + lax.rem(x + NX - o % NX, NX)

    def level(o):
        r, xd = lax.rem(row + o // NX, NR), lax.rem(x + o % NX, NX)
        return r * NX + xd, {"row": r, "col": z * NX + xd}

    load = pltpu.make_async_copy(g_hbm, gv, sem_g)
    load.start()
    load_row = pltpu.make_async_copy(row_hbm, row_old, sem_old.at[0])
    load_row.start()
    load_col = pltpu.make_async_copy(col_hbm, col_old, sem_old.at[1])
    load_col.start()
    load_weights = pltpu.make_async_copy(w_hbm, weights, sem_w)

    barrier = pltpu.get_barrier_semaphore()

    @pl.loop(1, NC)
    def _(o):
        pl.semaphore_signal(barrier, inc=1, device_id={"col": peer(o)}, device_id_type=MESH)

    @pl.loop(NX, NL)
    def _(o):
        pl.semaphore_signal(barrier, inc=1, device_id=level(o)[1], device_id_type=MESH)

    pl.semaphore_wait(barrier, NC - 1 + NL - NX)

    def block_cols(k):
        return pl.ds(pl.multiple_of(k * W, 128), W)

    def main_copy(k):
        return pltpu.make_async_remote_copy(
            src_ref=g_hbm.at[pl.ds(0, MAIN), block_cols(k)],
            dst_ref=main.at[me],
            send_sem=main_s.at[k],
            recv_sem=main_r.at[me],
            device_id={"col": k},
            device_id_type=MESH,
        )

    def main_wait(k):
        pltpu.make_async_copy(
            g_hbm.at[pl.ds(0, MAIN), pl.ds(0, W)], main.at[k], main_r.at[k]
        ).wait()

    def send_batch(n):
        first = 1 + sum(BATCHES[:n])

        @pl.loop(first, first + BATCHES[n])
        def _(j):
            main_copy(peer(lax.rem(j * STRIDE, NC))).start()

    def send_level(n, src, dst):
        @pl.loop(1, NL)
        def _(o):
            k, device = level(o)
            pltpu.make_async_remote_copy(
                src_ref=src(k),
                dst_ref=dst,
                send_sem=small_s.at[n],
                recv_sem=small_r.at[n],
                device_id=device,
                device_id_type=MESH,
            ).start()

    def send_z(n, ref):
        @pl.loop(1, NZ)
        def _(o):
            pltpu.make_async_remote_copy(
                src_ref=ref.at[z],
                dst_ref=ref.at[z],
                send_sem=small_s.at[n],
                recv_sem=small_r.at[n],
                device_id={"col": lax.rem(z + o, NZ) * NX + x},
                device_id_type=MESH,
            ).start()

    def wait_small(sem, ref, count):
        some = ref.at[pl.ds(0, count)]
        pltpu.make_async_copy(some, some, sem).wait()

    send_batch(0)

    load.wait()

    def add_up(k, carry):
        for c in range(CH):
            v = gv[:, pl.ds(pl.multiple_of(k * W + c * 128, 128), 128)].astype(F32)
            square = v * v
            part[k, c : c + 1, :] = jnp.sum(square, axis=0, keepdims=True)
            carry = carry + square
        return carry

    squares = lax.fori_loop(0, NC, add_up, jnp.zeros((SUB, 128), F32))

    parts[pl.ds(here, 1)] = part[pl.ds(here, 1)]
    send_level(0, lambda k: part.at[k], parts.at[here])

    sums_row = jnp.sum(squares, axis=1, keepdims=True)
    diagonal = lax.broadcasted_iota(jnp.int32, (SUB, 128), 0) == lax.broadcasted_iota(
        jnp.int32, (SUB, 128), 1
    )
    in_lanes = jnp.sum(
        jnp.where(diagonal, jnp.broadcast_to(sums_row, (SUB, 128)), 0.0), axis=0, keepdims=True
    )
    load_row.wait()
    moment = decay_rate * row_old[...] + (1.0 - decay_rate) * (
        in_lanes[:, :SUB] * (1.0 / FF) + tiny_value
    )
    rowm[...] = moment
    inv_out[...] = jnp.zeros_like(inv_out)
    inv_out[:, :SUB] = lax.rsqrt(moment)
    inv_in[pl.ds(me, 1)] = inv_out[...].reshape(1, 1, 128)

    def inv_copy(k):
        return pltpu.make_async_remote_copy(
            src_ref=inv_out,
            dst_ref=inv_in.at[me],
            send_sem=inv_s.at[k],
            recv_sem=inv_r.at[me],
            device_id={"col": k},
            device_id_type=MESH,
        )

    @pl.loop(1, NC)
    def _(o):
        inv_copy(peer(o)).start()

    def rest1_copy(zd):
        return pltpu.make_async_remote_copy(
            src_ref=pack1.at[zd],
            dst_ref=rest1.at[z],
            send_sem=r1_s.at[zd],
            recv_sem=r1_r.at[z],
            device_id={"col": zd * NX + x},
            device_id_type=MESH,
        )

    @pl.loop(0, NZ)
    def _(dz):
        zd = lax.rem(z + dz, NZ)
        for xd in range(NX):
            cols = pl.ds(pl.multiple_of((zd * NX + xd) * W, 128), W)
            stage1[xd * REST : (xd + 1) * REST, :] = gv[MAIN:SUB, cols].astype(F32)
        pack1[zd] = stage1[...].astype(BF16)

        @pl.when(dz != 0)
        def _():
            rest1_copy(zd).start()

        @pl.when(dz == 0)
        def _():
            rest1[zd] = stage1[...].astype(BF16)

    send_batch(1)
    load_weights.start()
    pltpu.make_async_copy(
        g_hbm.at[pl.ds(0, MAIN), block_cols(me)], main.at[me], main_r.at[me]
    ).start()
    load_col.wait()
    wait_small(small_r.at[0], parts, NL - 1)

    old = decay_rate * col_old[...] + (1.0 - decay_rate) * tiny_value
    old = jnp.where(z == row, old, jnp.zeros_like(old))
    zsums[pl.ds(z, 1)] = (jnp.sum(parts[...], axis=0) * ((1.0 - decay_rate) / D) + old)[None]
    send_z(1, zsums)
    send_batch(2)

    def rest2_copy(xd):
        return pltpu.make_async_remote_copy(
            src_ref=pack2.at[xd],
            dst_ref=rest2.at[x],
            send_sem=r2_s.at[xd],
            recv_sem=r2_r.at[x],
            device_id={"col": z * NX + xd},
            device_id_type=MESH,
        )

    wait_small(small_r.at[1], zsums, NZ - 1)

    moments[pl.ds(here, 1)] = jnp.sum(zsums[...], axis=0)[None]
    send_level(2, lambda k: moments.at[here], moments.at[here])
    send_batch(3)

    @pl.loop(1, NZ)
    def _(o):
        zs = lax.rem(z + o, NZ)
        pltpu.make_async_copy(pack1.at[zs], rest1.at[zs], r1_r.at[zs]).wait()

    for xd in range(NX):
        for zs in range(NZ):
            stage2[xd, zs * REST : (zs + 1) * REST, :] = rest1[zs].astype(F32)[
                xd * REST : (xd + 1) * REST, :
            ]

    wait_small(small_r.at[2], moments, NL - 1)
    colm[...] = moments[pl.ds(me, 1)].reshape(CH, 128)

    @pl.loop(0, NC)
    def _(k):
        inverse[k] = 1.0 / moments[k]

    def add_updates(k, carry):
        for c in range(CH):
            v = gv[:, pl.ds(pl.multiple_of(k * W + c * 128, 128), 128)].astype(F32)
            carry = carry + v * v * inverse[k, c : c + 1, :]
        return carry

    updates = lax.fori_loop(0, NC, add_updates, jnp.zeros((SUB, 128), F32))

    def as_column(line):
        column = jnp.sum(
            jnp.where(diagonal, jnp.broadcast_to(line, (SUB, 128)), 0.0), axis=1, keepdims=True
        )
        return jnp.broadcast_to(column, (SUB, 128))

    mine = as_column(inv_out[...])
    lines[pl.ds(here, 1)] = jnp.sum(updates * (mine * mine), axis=0, keepdims=True)[None]
    send_level(3, lambda k: lines.at[here], lines.at[here])
    send_batch(4)

    @pl.loop(0, NX)
    def _(xd):
        pack2[xd] = stage2[xd].astype(BF16)

        @pl.when(xd != x)
        def _():
            rest2_copy(xd).start()

        @pl.when(xd == x)
        def _():
            rest2[xd] = stage2[xd].astype(BF16)

    wait_small(small_r.at[3], lines, NL - 1)

    zlines[pl.ds(z, 1)] = jnp.sum(lines[...], axis=0)[None]
    send_z(4, zlines)
    send_batch(5)

    @pl.loop(0, NC)
    def _(k):
        @pl.when(k != me)
        def _():
            pltpu.make_async_copy(inv_out, inv_in.at[k], inv_r.at[k]).wait()

        inv_col[k] = as_column(inv_in[pl.ds(k, 1)].reshape(1, 128))

    load_weights.wait()

    @pl.loop(1, NC)
    def _(o):
        inv_copy(peer(o)).wait_send()

    @pl.loop(1, NZ)
    def _(o):
        rest1_copy(lax.rem(z + o, NZ)).wait_send()

    @pl.loop(1, NX)
    def _(o):
        rest2_copy(lax.rem(x + o, NX)).wait_send()

    wait_small(small_s.at[0], parts, NL - 1)
    wait_small(small_s.at[1], zsums, NZ - 1)
    wait_small(small_s.at[2], moments, NL - 1)
    wait_small(small_s.at[3], lines, NL - 1)
    wait_small(small_s.at[4], zlines, NZ - 1)
    wait_small(small_r.at[4], zlines, NZ - 1)

    square_sum = jnp.sum(jnp.sum(zlines[...], axis=0), axis=1, keepdims=True)
    factor = 1.0 / jnp.maximum(1.0, jnp.sqrt(square_sum / (D * FF)) / clip_limit)
    scale = (step_size * factor) * lax.rsqrt(colm[...])

    def finish(j):
        k = source(lax.rem(j * STRIDE, NC))
        main_wait(k)
        p = k // 2
        for e in range(2):

            @pl.when(k % 2 == e)
            def _():
                rows = slice(e * SUB, e * SUB + MAIN)
                for c, lanes in lane_slices():
                    v = main[k, :, lanes].astype(F32) * inv_col[k, :MAIN, :]
                    done[p, rows, lanes] = weights[p, rows, lanes] - scale[c : c + 1, :] * v

    @pl.loop(0, NC - 8)
    def _(j):
        finish(j)

    @pl.loop(0, NX)
    def _(xs):
        @pl.when(xs != x)
        def _():
            pltpu.make_async_copy(pack2.at[xs], rest2.at[xs], r2_r.at[xs]).wait()

    for c, lanes in lane_slices():
        for xs in range(NX):
            values = rest2[xs, :, lanes].astype(F32)
            at = (xs % 2) * SUB + MAIN
            rows = slice(at, at + REST)
            for zs in range(NZ):
                v = values[zs * REST : (zs + 1) * REST, :] * inv_col[zs * NX + xs, MAIN:SUB, :]
                p = zs * 2 + xs // 2
                done[p, rows, lanes] = weights[p, rows, lanes] - scale[c : c + 1, :] * v

    @pl.loop(NC - 8, NC)
    def _(j):
        finish(j)

    @pl.loop(1, NC)
    def _(o):
        main_copy(peer(o)).wait_send()


def write_kernel(done, colm_in, rowm_in, out_hbm, colm, rowm, sem):
    @pl.loop(0, NP)
    def _(p):
        pltpu.make_async_copy(done.at[p], out_hbm.at[p], sem.at[p]).start()

    colm[...] = colm_in[...]
    rowm[...] = rowm_in[...]

    @pl.loop(0, NP)
    def _(p):
        pltpu.make_async_copy(done.at[p], out_hbm.at[p], sem.at[p]).wait()


def local(gradient, weights, row_old, col_old):
    vmem = pl.BlockSpec(memory_space=pltpu.VMEM)
    hbm = pl.BlockSpec(memory_space=pltpu.HBM)
    dma = pltpu.SemaphoreType.DMA
    arrays = (
        gradient, weights.reshape(NP, PAIR, W), row_old.reshape(1, SUB), col_old.reshape(CH, 128)
    )
    done, colm, rowm = pl.pallas_call(
        gather_kernel,
        out_shape=(
            pltpu.VMEM((NP, PAIR, W), F32),
            pltpu.VMEM((CH, 128), F32),
            pltpu.VMEM((1, SUB), F32),
        ),
        in_specs=[hbm] * 4,
        out_specs=(vmem,) * 3,
        scratch_shapes=[
            pltpu.VMEM((NP, PAIR, W), F32),
            pltpu.VMEM((1, SUB), F32),
            pltpu.VMEM((CH, 128), F32),
            pltpu.VMEM((SUB, FF), BF16),
            pltpu.VMEM((NC, MAIN, W), BF16),
            pltpu.VMEM((NZ, NX * REST, W), BF16),
            pltpu.VMEM((NZ, NX * REST, W), BF16),
            pltpu.VMEM((NX, NZ * REST, W), BF16),
            pltpu.VMEM((NX, NZ * REST, W), BF16),
            pltpu.VMEM((NX * REST, W), F32),
            pltpu.VMEM((NX, NZ * REST, W), F32),
            pltpu.VMEM((1, 128), F32),
            pltpu.VMEM((NC, 1, 128), F32),
            pltpu.VMEM((NC, SUB, 128), F32),
            pltpu.VMEM((NC, CH, 128), F32),
            pltpu.VMEM((NL, CH, 128), F32),
            pltpu.VMEM((NZ, CH, 128), F32),
            pltpu.VMEM((NL, CH, 128), F32),
            pltpu.VMEM((NC, CH, 128), F32),
            pltpu.VMEM((NL, 1, 128), F32),
            pltpu.VMEM((NZ, 1, 128), F32),
            dma, dma, dma((2,)), dma((NC,)), dma((NC,)), dma((NC,)), dma((NC,)),
            dma((NZ,)), dma((NZ,)), dma((NX,)), dma((NX,)), dma((5,)), dma((5,)),
        ],
        compiler_params=pltpu.CompilerParams(
            collective_id=0, has_side_effects=True, vmem_limit_bytes=28 * 2**20
        ),
        cost_estimate=pl.CostEstimate(
            flops=8 * SUB * FF, bytes_accessed=4 * SUB * FF, transcendentals=0
        ),
        name="gather_kernel",
    )(*[pltpu.with_memory_space_constraint(a, pltpu.HBM) for a in arrays])
    new_weights, colm, rowm = pl.pallas_call(
        write_kernel,
        out_shape=(
            jax.ShapeDtypeStruct((NP, PAIR, W), F32),
            jax.ShapeDtypeStruct((CH, 128), F32),
            jax.ShapeDtypeStruct((1, SUB), F32),
        ),
        in_specs=[vmem] * 3,
        out_specs=(hbm, vmem, vmem),
        scratch_shapes=[dma((NP,))],
        compiler_params=pltpu.CompilerParams(vmem_limit_bytes=2**20),
        cost_estimate=pl.CostEstimate(
            flops=2 * SUB * FF, bytes_accessed=4 * SUB * FF, transcendentals=0
        ),
        name="write_kernel",
    )(done, colm, rowm)
    return (new_weights.reshape(SUB * NC, W), rowm.reshape(SUB), colm.reshape(W))


def solution(mesh):
    in_specs = (P(("row", "col"), None), P("row", "col"), P(("row", "col")), P("col"))
    out_specs = (P("row", "col"), P(("row", "col")), P("col"))
    return jax.shard_map(local, mesh=mesh, in_specs=in_specs, out_specs=out_specs, check_vma=False)
```

time: 268 us -> 78.7 us (0.29)
  blocking collectives: 160 us -> 0 us
  Pallas kernels: 0 us -> 77.2 us
  waiting for transfers between devices: 66.5 us -> 0 us
  other arithmetic: 15.2 us -> 0 us
  local copies, waits for them, and re-layouts: 12.4 us -> 0 us
  starting transfers between devices: 12 us -> 0 us
    psum x3 -> x0, blocking collectives: 160 us -> none  [the longest x1 72.6 us: finish(): square_sum = lax.psum(jnp.sum(update * update), ('row', 'col'))]
    pallas_call x0 -> x2, Pallas kernels: none -> 77.2 us  [the longest x1 74.1 us: local(): pl.pallas_call(gather_kernel, out_shape=(pltpu.VMEM((NP, PAIR, W), F32),...]
    all_to_all x1 -> x0, waiting for transfers between devices: 66.5 us -> none  [local(): lax.all_to_all(gradient, 'col', split_axis=1, concat_axis=0, tiled=True)]
    all_to_all x1 -> x0, starting transfers between devices: 12 us -> none  [local(): lax.all_to_all(gradient, 'col', split_axis=1, concat_axis=0, tiled=True)]
    sub x1 -> x0, other arithmetic: 7.4 us -> none  [local(): new_weights = weights - step_size * factor * update]
    convert_element_type x1 -> x0, local copies, waits for them, and re-layouts: 6.68 us -> none  [local(): values = blocked.astype(jnp.float32)]
    reduce_sum x2 -> x0, other arithmetic: 4.71 us -> none  [the longest x1 3.14 us: finish(): square_sum = lax.psum(jnp.sum(update * update), ('row', 'col'))]
    convert_element_type x1 -> x0, other arithmetic: 2.9 us -> none  [local(): values = blocked.astype(jnp.float32)]
  transfers between devices with their start and end apart: 1 -> 0, of which waited for: 1 -> 0; matrix products, arithmetic and copies ran while one was open for 0% -> 0% of each run, Pallas kernels for 0% -> 0%
where the time goes in v2:
time: 78.7 us; the launch traced here: 77.8 us
  Pallas kernels  77.2 us (98%)
    pallas_call x1, Pallas kernels, local(): pl.pallas_call(gather_kernel, out_shape=(pltpu.VMEM((NP, PAIR, W), F32),...  74.1 us
    pallas_call x1, Pallas kernels, local(): pl.pallas_call(write_kernel, out_shape=(jax.ShapeDtypeStruct((NP, PAIR, W...  3.09 us

profile of v2, /device:TPU:1, one launch (start us, length us, event | category | flops | bytes accessed | tf_op | source)
XLA Modules:
  0.0 77.8 jit_solution(1069117371434218806)
XLA Ops:
  0.6 74.1 %gather_kernel.1 = (f32[16,72,1152]{2,1,0:T(8,128)S(1)}, f32[9,128]{1,0:T(8,128)S(1)}, f32[1,36]{1,0:T(1,128)S(1)}) custom-call(bf16[36,36864]{1,0:T(8,128)(2,1)} %g_hbm.1, f32[16,72,1152]{2,1,0:T(8,128)} %bitcast.6, f32[1,36]{1,0:T(1,128)} %bitcast.8, f32[9,128]{1,0:T(8,128)} %bitcast.7), custom_call_target="tpu_custom_call" | custom-call | flops 10616832 | bytes 5308416 | tf_op jit(solution)/shard_map/gather_kernel/pallas_call | solution.py:387
  74.7 3.1 %write_kernel.1 = (f32[16,72,1152]{2,1,0:T(8,128)}, f32[9,128]{1,0:T(8,128)}, f32[1,36]{1,0:T(1,128)}) custom-call(f32[16,72,1152]{2,1,0:T(8,128)S(1)} %get-tuple-element.9.done, f32[9,128]{1,0:T(8,128)S(1)} %get-tuple-element.10.colm_in, f32[1,36]{1,0:T(1,128)S(1)} %get-tuple-element.11.rowm_in), custom_call_target="tpu_custom_call" | custom-call | flops 2654208 | bytes 5308416 | tf_op jit(solution)/shard_map/write_kernel/pallas_call | solution.py:429

commit v3 on v2

--- a/solution.py
+++ b/solution.py
@@ -24,8 +24,8 @@
 CH = W // 128
 PAIR = 2 * SUB
 NP = NC // 2
-STRIDE = 13
-BATCHES = (6, 5, 5, 5, 5, 5)
+ORDER = (0,13, 26, 7, 20, 14, 27, 8, 21, 15, 28, 9, 22, 16, 29, 10, 23, 4, 17, 30, 11, 24, 5, 18, 31, 12, 25, 6, 19, 1, 2, 3)
+BATCHES = (6, 6, 6, 5, 4, 4)
 F32 = jnp.float32
 BF16 = jnp.bfloat16
 MESH = pl.DeviceIdType.MESH
@@ -53,9 +53,34 @@
     def source(o):
         return lax.rem(z + NZ - o // NX, NZ) * NX + lax.rem(x + NX - o % NX, NX)
 
+    def offset(j):
+        o = 0
+        for i in range(1, NC):
+            o = jnp.where(j == i, ORDER[i], o)
+        return o
+
     def level(o):
         r, xd = lax.rem(row + o // NX, NR), lax.rem(x + o % NX, NX)
         return r * NX + xd, {"row": r, "col": z * NX + xd}
+
+    barrier = pltpu.get_barrier_semaphore()
+    z_at = [lax.rem(z + d, NZ) * NX for d in range(NZ)]
+    x_at = [lax.rem(x + d, NX) for d in range(NX)]
+    r_at = [lax.rem(row + d, NR) for d in range(NR)]
+
+    def far(d, n):
+        return min(d, n - d)
+
+    near = [(0, dz, dx) for dz in range(NZ) for dx in range(NX) if dz or dx]
+    near += [(dr, 0, dx) for dr in range(1, NR) for dx in range(NX)]
+    near.sort(key=lambda o: -far(o[0], NR) // 2 - far(o[1], NZ) - far(o[2], NX))
+    for dr, dz, dx in near:
+        pl.semaphore_signal(
+            barrier,
+            inc=1,
+            device_id={"row": r_at[dr], "col": z_at[dz] + x_at[dx]},
+            device_id_type=MESH,
+        )
 
     load = pltpu.make_async_copy(g_hbm, gv, sem_g)
     load.start()
@@ -64,16 +89,6 @@
     load_col = pltpu.make_async_copy(col_hbm, col_old, sem_old.at[1])
     load_col.start()
     load_weights = pltpu.make_async_copy(w_hbm, weights, sem_w)
-
-    barrier = pltpu.get_barrier_semaphore()
-
-    @pl.loop(1, NC)
-    def _(o):
-        pl.semaphore_signal(barrier, inc=1, device_id={"col": peer(o)}, device_id_type=MESH)
-
-    @pl.loop(NX, NL)
-    def _(o):
-        pl.semaphore_signal(barrier, inc=1, device_id=level(o)[1], device_id_type=MESH)
 
     pl.semaphore_wait(barrier, NC - 1 + NL - NX)
 
@@ -100,7 +115,7 @@
 
         @pl.loop(first, first + BATCHES[n])
         def _(j):
-            main_copy(peer(lax.rem(j * STRIDE, NC))).start()
+            main_copy(peer(offset(j))).start()
 
     def send_level(n, src, dst):
         @pl.loop(1, NL)
@@ -245,6 +260,18 @@
                 xd * REST : (xd + 1) * REST, :
             ]
 
+    @pl.loop(0, NX)
+    def _(xd):
+        pack2[xd] = stage2[xd].astype(BF16)
+
+        @pl.when(xd != x)
+        def _():
+            rest2_copy(xd).start()
+
+        @pl.when(xd == x)
+        def _():
+            rest2[xd] = stage2[xd].astype(BF16)
+
     wait_small(small_r.at[2], moments, NL - 1)
     colm[...] = moments[pl.ds(me, 1)].reshape(CH, 128)
 
@@ -270,18 +297,6 @@
     lines[pl.ds(here, 1)] = jnp.sum(updates * (mine * mine), axis=0, keepdims=True)[None]
     send_level(3, lambda k: lines.at[here], lines.at[here])
     send_batch(4)
-
-    @pl.loop(0, NX)
-    def _(xd):
-        pack2[xd] = stage2[xd].astype(BF16)
-
-        @pl.when(xd != x)
-        def _():
-            rest2_copy(xd).start()
-
-        @pl.when(xd == x)
-        def _():
-            rest2[xd] = stage2[xd].astype(BF16)
 
     wait_small(small_r.at[3], lines, NL - 1)
 
@@ -323,7 +338,13 @@
     scale = (step_size * factor) * lax.rsqrt(colm[...])
 
     def finish(j):
-        k = source(lax.rem(j * STRIDE, NC))
+        at = offset(j)
+        k = source(at)
+
+        @pl.when(j > 0)
+        def _():
+            main_copy(peer(at)).wait_send()
+
         main_wait(k)
         p = k // 2
         for e in range(2):
@@ -359,22 +380,17 @@
     def _(j):
         finish(j)
 
-    @pl.loop(1, NC)
-    def _(o):
-        main_copy(peer(o)).wait_send()
-
-
-def write_kernel(done, colm_in, rowm_in, out_hbm, colm, rowm, sem):
-    @pl.loop(0, NP)
-    def _(p):
-        pltpu.make_async_copy(done.at[p], out_hbm.at[p], sem.at[p]).start()
-
-    colm[...] = colm_in[...]
-    rowm[...] = rowm_in[...]
-
-    @pl.loop(0, NP)
-    def _(p):
-        pltpu.make_async_copy(done.at[p], out_hbm.at[p], sem.at[p]).wait()
+
+def write_kernel(done, colm, rowm, done_hbm, colm_hbm, rowm_hbm, sem):
+    copies = [
+        pltpu.make_async_copy(done, done_hbm, sem.at[0]),
+        pltpu.make_async_copy(colm, colm_hbm, sem.at[1]),
+        pltpu.make_async_copy(rowm, rowm_hbm, sem.at[2]),
+    ]
+    for copy in copies:
+        copy.start()
+    for copy in copies:
+        copy.wait()
 
 
 def local(gradient, weights, row_old, col_old):
@@ -434,8 +450,8 @@
             jax.ShapeDtypeStruct((1, SUB), F32),
         ),
         in_specs=[vmem] * 3,
-        out_specs=(hbm, vmem, vmem),
-        scratch_shapes=[dma((NP,))],
+        out_specs=(hbm,) * 3,
+        scratch_shapes=[dma((3,))],
         compiler_params=pltpu.CompilerParams(vmem_limit_bytes=2**20),
         cost_estimate=pl.CostEstimate(
             flops=2 * SUB * FF, bytes_accessed=4 * SUB * FF, transcendentals=0

time: 78.7 us -> 77.2 us (0.981)
  no operation moved by 1% of the time
where the time goes in v3:
time: 77.2 us; the launch traced here: 77.1 us
  Pallas kernels  76.5 us (99%)
    pallas_call x1, Pallas kernels, local(): pl.pallas_call(gather_kernel, out_shape=(pltpu.VMEM((NP, PAIR, W), F32),...  74.1 us
    pallas_call x1, Pallas kernels, local(): pl.pallas_call(write_kernel, out_shape=(jax.ShapeDtypeStruct((NP, PAIR, W...  2.41 us

profile of v3, /device:TPU:1, one launch (start us, length us, event | category | flops | bytes accessed | tf_op | source)
XLA Modules:
  0.0 77.1 jit_solution(17114415290237123955)
XLA Ops:
  0.6 74.1 %gather_kernel.1 = (f32[16,72,1152]{2,1,0:T(8,128)S(1)}, f32[9,128]{1,0:T(8,128)S(1)}, f32[1,36]{1,0:T(1,128)S(1)}) custom-call(bf16[36,36864]{1,0:T(8,128)(2,1)} %g_hbm.1, f32[16,72,1152]{2,1,0:T(8,128)} %bitcast.6, f32[1,36]{1,0:T(1,128)} %bitcast.8, f32[9,128]{1,0:T(8,128)} %bitcast.7), custom_call_target="tpu_custom_call" | custom-call | flops 10616832 | bytes 5308416 | tf_op jit(solution)/shard_map/gather_kernel/pallas_call | solution.py:403
  74.7 2.4 %write_kernel.1 = (f32[16,72,1152]{2,1,0:T(8,128)}, f32[9,128]{1,0:T(8,128)}, f32[1,36]{1,0:T(1,128)}) custom-call(f32[16,72,1152]{2,1,0:T(8,128)S(1)} %get-tuple-element.9.done, f32[9,128]{1,0:T(8,128)S(1)} %get-tuple-element.10.colm, f32[1,36]{1,0:T(1,128)S(1)} %get-tuple-element.11.rowm), custom_call_target="tpu_custom_call" | custom-call | flops 2654208 | bytes 5308416 | tf_op jit(solution)/shard_map/write_kernel/pallas_call | solution.py:445

commit v4 on v3

--- a/solution.py
+++ b/solution.py
@@ -189,10 +189,6 @@
             device_id_type=MESH,
         )
 
-    @pl.loop(1, NC)
-    def _(o):
-        inv_copy(peer(o)).start()
-
     def rest1_copy(zd):
         return pltpu.make_async_remote_copy(
             src_ref=pack1.at[zd],
@@ -232,6 +228,11 @@
     zsums[pl.ds(z, 1)] = (jnp.sum(parts[...], axis=0) * ((1.0 - decay_rate) / D) + old)[None]
     send_z(1, zsums)
     send_batch(2)
+
+    @pl.loop(1, NC)
+    def _(o):
+        inv_copy(peer(o)).start()
+
 
     def rest2_copy(xd):
         return pltpu.make_async_remote_copy(

time: 77.2 us -> 77.2 us (level)
  no operation moved by 1% of the time
where the time goes in v4:
time: 77.2 us; the launch traced here: 77.1 us
  Pallas kernels  76.5 us (99%)
    pallas_call x1, Pallas kernels, local(): pl.pallas_call(gather_kernel, out_shape=(pltpu.VMEM((NP, PAIR, W), F32),...  74.1 us
    pallas_call x1, Pallas kernels, local(): pl.pallas_call(write_kernel, out_shape=(jax.ShapeDtypeStruct((NP, PAIR, W...  2.41 us

profile of v4, /device:TPU:1, one launch (start us, length us, event | category | flops | bytes accessed | tf_op | source)
XLA Modules:
  0.0 77.1 jit_solution(12727403713525048164)
XLA Ops:
  0.6 74.1 %gather_kernel.1 = (f32[16,72,1152]{2,1,0:T(8,128)S(1)}, f32[9,128]{1,0:T(8,128)S(1)}, f32[1,36]{1,0:T(1,128)S(1)}) custom-call(bf16[36,36864]{1,0:T(8,128)(2,1)} %g_hbm.1, f32[16,72,1152]{2,1,0:T(8,128)} %bitcast.6, f32[1,36]{1,0:T(1,128)} %bitcast.8, f32[9,128]{1,0:T(8,128)} %bitcast.7), custom_call_target="tpu_custom_call" | custom-call | flops 10616832 | bytes 5308416 | tf_op jit(solution)/shard_map/gather_kernel/pallas_call | solution.py:404
  74.7 2.4 %write_kernel.1 = (f32[16,72,1152]{2,1,0:T(8,128)}, f32[9,128]{1,0:T(8,128)}, f32[1,36]{1,0:T(1,128)}) custom-call(f32[16,72,1152]{2,1,0:T(8,128)S(1)} %get-tuple-element.9.done, f32[9,128]{1,0:T(8,128)S(1)} %get-tuple-element.10.colm, f32[1,36]{1,0:T(1,128)S(1)} %get-tuple-element.11.rowm), custom_call_target="tpu_custom_call" | custom-call | flops 2654208 | bytes 5308416 | tf_op jit(solution)/shard_map/write_kernel/pallas_call | solution.py:446
